TPU v7x, 32 devices: a whole 2x2x4 slice. The times are simulated.
32 devices in a mesh: co: 16 (over z, y, core), ci: 2 (over x).
Axes of the slice: x: 2, y: 2, z: 4, core: 2. Of those that a mesh axis runs over, the one named last changes fastest.
Arguments:
- features: bfloat16 [1024, 1024], P('ci'), may hold values from -6 to 6
- filter_bank: bfloat16 [27, 1024, 1024], P(None, 'co', 'ci'), may hold values from -0.0390625 to 0.0390625
- out_grad: bfloat16 [1024, 1024], P('co', 'ci'), may hold values from -6 to 6
Outputs:
- response: bfloat16 [1024, 1024], P('co', 'ci')
- in_grad: bfloat16 [1024, 1024], P('ci', 'co')
- filter_grad: float32 [27, 1024, 1024], P(None, 'co', 'ci')
All inputs are finite; a program needn't handle non-finite values.
Results may differ from a plain program's by a relative error of at most 0.001.
Values may be sent and summed in bfloat16 or wider, within the bound.
A program may use at most 64 MiB of HBM per device.

v0:
```python
import jax
import jax.numpy as jnp
from jax import lax
from jax.sharding import PartitionSpec as P

NY = 8
NZ = 8


def body(features, filter_bank, out_grad):
    chan_in, cell_count = features.shape
    chan_out = filter_bank.shape[1]
    planes = cell_count // (NY * NZ)
    pads = ((1, 1), (1, 1), (1, 1))
    volume = features.reshape(1, chan_in, planes, NY, NZ)
    kernel = filter_bank.reshape(3, 3, 3, chan_out, chan_in)
    partial_value = lax.conv_general_dilated(
        volume,
        kernel,
        (1, 1, 1),
        pads,
        dimension_numbers=("NCDHW", "DHWOI", "NCDHW"),
        preferred_element_type=jnp.float32,
    )
    partial_value = partial_value.reshape(chan_out, cell_count)
    response = lax.psum_scatter(partial_value, "ci", scatter_dimension=1, tiled=True).astype(
        jnp.bfloat16
    )
    grad_full = lax.all_gather(out_grad, "ci", axis=1, tiled=True)
    weight_terms = lax.conv_general_dilated(
        features.reshape(chan_in, 1, planes, NY, NZ),
        grad_full.reshape(chan_out, 1, planes, NY, NZ),
        (1, 1, 1),
        pads,
        dimension_numbers=("NCDHW", "OIDHW", "NCDHW"),
        preferred_element_type=jnp.float32,
    )
    scale = float(cell_count) ** (-0.5)
    filter_grad = (weight_terms * scale).transpose(2, 3, 4, 1, 0).reshape(27, chan_out, chan_in)
    flipped = kernel[::-1, ::-1, ::-1]
    grad_terms = lax.conv_general_dilated(
        grad_full.reshape(1, chan_out, planes, NY, NZ),
        flipped,
        (1, 1, 1),
        pads,
        dimension_numbers=("NCDHW", "DHWIO", "NCDHW"),
        preferred_element_type=jnp.float32,
    )
    grad_terms = grad_terms.reshape(chan_in, cell_count)
    in_grad = lax.psum_scatter(grad_terms, "co", scatter_dimension=1, tiled=True).astype(
        jnp.bfloat16
    )
    return (response, in_grad, filter_grad)


def solution(mesh):
    placed = (P("ci", None), P(None, "co", "ci"), P("co", "ci"))
    return jax.shard_map(
        body,
        mesh=mesh,
        in_specs=placed,
        out_specs=(P("co", "ci"), P("ci", "co"), P(None, "co", "ci")),
        check_vma=False,
    )
```

profile of v0, /device:TPU:0, one launch (start us, length us, event | category | flops | bytes accessed | tf_op | source)
XLA Modules:
  0.0 124.6 jit_solution(13638596001435200401)
XLA Ops:
  7.2 0.0 copy-start
  7.2 0.0 reduce-scatter.3.cloned.1.call-start
  7.2 1.6 %copy.11 = bf16[512,1024]{0,1:T(8,128)(2,1)S(1)} copy(bf16[512,1024]{1,0:T(8,128)(2,1)} %param.3) | data formatting | bytes 2097152 | tf_op args[0]
  8.9 0.1 copy-done
  9.0 0.0 copy-start.1
  9.0 20.4 %fusion.2 = f32[1,64,16,8,8]{1,0,4,3,2:T(1,128)S(1)} fusion(bf16[3,3,3,64,512]{4,3,2,1,0:T(8,128)(2,1)S(1)} %bitcast.10, bf16[1,512,16,8,8]{1,4,3,2,0:T(8,128)(2,1)S(1)} %bitcast.13), kind=kOutput, calls=%fused_computation.2 | convolution fusion | flops 1459093504 | bytes 3080192 | tf_op jit(solution)/shard_map/conv_general_dilated | solution.py:17
  29.4 0.9 copy.13
  30.3 0.0 reduce-scatter.3.cloned.1.call-update
  30.3 0.0 reduce-scatter.5.cloned.1.call-start
  30.4 0.0 copy-done.1
  30.4 0.1 copy.14
  30.5 7.3 %all_gather.3 = bf16[64,1024]{0,1:T(8,128)(2,1)S(1)} all-gather(bf16[64,512]{0,1:T(8,128)(2,1)S(1)} %copy.14), channel_id=1, replica_groups=mesh['co'=16,'ci'=2] {'ci'}, dimensions={1}, use_global_device_ids=true | all-gather | bytes 196608 | tf_op jit(solution)/shard_map/all_gather | solution.py:29
  37.8 13.6 %fusion.8 = f32[1,512,16,8,8]{1,0,4,3,2:T(1,128)S(1)} fusion(bf16[3,3,3,64,512]{4,3,2,1,0:T(8,128)(2,1)S(1)} %bitcast.11, bf16[1,64,16,8,8]{1,4,3,2,0:T(8,128)(2,1)S(1)} %bitcast.16), kind=kOutput, calls=%fused_computation.6 | convolution fusion | flops 1459093504 | bytes 3997696 | tf_op jit(solution)/shard_map/conv_general_dilated | solution.py:41
  51.4 1.6 %copy.19 = f32[1,512,16,8,8]{1,4,0,3,2:T(8,128)} copy(f32[1,512,16,8,8]{1,0,4,3,2:T(1,128)S(1)} %fusion.8) | data formatting | bytes 4194304
  53.0 0.0 reduce-scatter.5.cloned.1.call-update
  53.0 28.4 %fusion.4 = f32[3,3,3,64,512]{4,3,2,1,0:T(8,128)} fusion(bf16[512,1,16,8,8]{0,4,3,2,1:T(8,128)(2,1)S(1)} %bitcast.14, bf16[64,1,16,8,8]{0,4,3,2,1:T(8,128)(2,1)S(1)} %bitcast.17), kind=kOutput, calls=%fused_computation.4 | convolution fusion | flops 1459978240 | bytes 4718592 | tf_op jit(solution)/shard_map/conv_general_dilated | solution.py:30
  81.4 0.0 reduce-scatter.3.cloned.1.call-done
  81.4 1.6 %convert_element_type.6 = bf16[64,512]{1,0:T(8,128)(2,1)} convert(f32[64,512]{1,0:T(8,128)} %reduce-scatter.3.cloned.1.call-done) | non-fusion elementwise | flops 32768 | bytes 196608 | tf_op jit(solution)/shard_map/convert_element_type | solution.py:26
  82.9 33.3 %reduce-scatter.5.cloned.1.call-done = f32[512,64]{0,1:T(8,128)} async-done(((f32[512,1024]{0,1:T(8,128)}), f32[512,64]{0,1:T(8,128)}) %reduce-scatter.5.cloned.1.call-update) | async-done | bytes 131088 | tf_op jit(solution)/shard_map/reduce_scatter | solution.py:50
  116.3 1.5 %convert_element_type.7 = bf16[512,64]{0,1:T(8,128)(2,1)} convert(f32[512,64]{0,1:T(8,128)} %reduce-scatter.5.cloned.1.call-done) | non-fusion elementwise | flops 32768 | bytes 196608 | tf_op jit(solution)/shard_map/convert_element_type | solution.py:50
Async XLA Ops:
  7.2 1.8 %copy-start = (bf16[27,64,512]{2,1,0:T(8,128)(2,1)S(1)}, bf16[27,64,512]{2,1,0:T(8,128)(2,1)}, u32[]{:S(2)}) copy-start(bf16[27,64,512]{2,1,0:T(8,128)(2,1)} %param.4) | copy-start | bytes 5308420
  7.2 74.2 %reduce-scatter.3.cloned.1.call-start = ((), (), s32[]{:S(2)}) async-start(), calls=%async_computation.2 | async-start | bytes 393216 | tf_op jit(solution)/shard_map/reduce_scatter | solution.py:26
  9.0 21.4 %copy-start.1 = (bf16[64,512]{1,0:T(8,128)(2,1)S(1)}, bf16[64,512]{1,0:T(8,128)(2,1)}, u32[]{:S(2)}) copy-start(bf16[64,512]{1,0:T(8,128)(2,1)} %param.5) | copy-start | bytes 196612
  30.3 85.9 %reduce-scatter.5.cloned.1.call-start = ((), (), s32[]{:S(2)}) async-start(), calls=%async_computation.3 | async-start | bytes 2228224 | tf_op jit(solution)/shard_map/reduce_scatter | solution.py:50
Sparse Core Ops, SparseCore 0:
  30.5 14.3 reduce-scatter.2
  53.1 63.0 reduce-scatter.4
where the time goes:
time: 125 us
  matrix products  62.4 us (50%)
  waiting for transfers between devices  33.4 us (27%)
  between operations  14.1 us (11%)
  blocking collectives  7.27 us (6%)
  local copies, waits for them, and re-layouts  4.36 us (3%)
  other arithmetic  3.09 us (2%)
    reduce_scatter x1, waiting for transfers between devices, body(): lax.psum_scatter(grad_terms, 'co', scatter_dimension=1, tiled=True)  33.3 us
    conv_general_dilated x1, matrix products, body(): lax.conv_general_dilated(features.reshape(chan_in, 1, planes, NY, NZ), gr...  28.4 us
    conv_general_dilated x1, matrix products, body(): lax.conv_general_dilated(volume, kernel, (1, 1, 1), pads, dimension_numbe...  20.4 us
    conv_general_dilated x1, matrix products, body(): lax.conv_general_dilated(grad_full.reshape(1, chan_out, planes, NY, NZ),...  13.6 us
    all_gather x1, blocking collectives, body(): grad_full = lax.all_gather(out_grad, 'ci', axis=1, tiled=True)  7.27 us
    unnamed x7, local copies, waits for them, and re-layouts  3.45 us
  transfers between devices with their start and end apart: 2, of which 1 were waited for; matrix products, arithmetic and copies ran while one was open for 36% of the time, Pallas kernels for 0%

commit v1 on v0

v1 whole, which is shorter than its diff:
```python
import functools

import jax
import jax.numpy as jnp
from jax import lax
from jax.experimental import pallas as pl
from jax.experimental.pallas import tpu as pltpu
from jax.sharding import PartitionSpec as P

NY = 8
NZ = 8
PLANE = NY * NZ
LANES = 128
MESH = pl.DeviceIdType.MESH


def place(plane, order):
    spot = 0
    for bit in order:
        spot = spot * 2 + (plane >> bit) % 2
    return spot


def kernel(
    n_co, n_ci, orders,
    f_hbm, w_hbm, g_hbm,
    resp_ref, ingrad_ref, fg_hbm,
    f_ref, w_ref, g_ref, base, acc, recvs, ysum, rpart, rrecv, u_mid, u_side, fg_ref,
    in_sem, gs_sem, gr_sem, rs_sem, rr_sem, hs_sem, hr_sem, out_sem,
):
    cells = f_ref.shape[1]
    ci_n = f_ref.shape[0]
    co_n, half = g_ref.shape[1], g_ref.shape[2]
    planes = cells // PLANE
    rows_w = 27 * co_n
    depth = 3 * co_n
    wide = base.shape[2]
    stages = len(orders[0])
    chunks = len(orders)
    co_me = lax.axis_index("co")
    ci_me = lax.axis_index("ci")

    def co_bit(bit):
        return lax.rem(co_me // (1 << bit), 2)

    def co_partner(bit):
        return co_me + (1 - 2 * co_bit(bit)) * (1 << bit)

    def ci_other(d):
        return lax.rem(ci_me + d, n_ci)

    load_w = pltpu.make_async_copy(w_hbm, w_ref.at[pl.ds(0, rows_w)], in_sem.at[0])
    load_f = pltpu.make_async_copy(f_hbm, f_ref, in_sem.at[1])
    load_g = pltpu.make_async_copy(g_hbm, g_ref.at[ci_me], in_sem.at[2])
    load_w.start()
    load_f.start()
    load_g.start()

    barrier = pltpu.get_barrier_semaphore()
    for bit in range(stages):
        pl.semaphore_signal(barrier, inc=1, device_id={"co": co_partner(bit)}, device_id_type=MESH)
    for d in range(1, n_ci):
        pl.semaphore_signal(barrier, inc=1, device_id={"ci": ci_other(d)}, device_id_type=MESH)
    pl.semaphore_wait(barrier, stages + n_ci - 1)

    g_copies = []
    for d in range(1, n_ci):
        copy = pltpu.make_async_remote_copy(
            src_ref=g_hbm, dst_ref=g_ref.at[ci_me],
            send_sem=gs_sem.at[d - 1], recv_sem=gr_sem.at[d - 1],
            device_id={"ci": ci_other(d)}, device_id_type=MESH,
        )
        copy.start()
        g_copies.append(copy)

    w_ref[rows_w:, :] = jnp.zeros((w_ref.shape[0] - rows_w, ci_n), w_ref.dtype)
    base[:, 0:PLANE, :] = jnp.zeros((3, PLANE, wide), base.dtype)
    base[:, PLANE + cells:, :] = jnp.zeros((3, PLANE, wide), base.dtype)
    load_w.wait()
    load_f.wait()

    tile = 2 * LANES

    def response_tile(at):
        lane = lax.broadcasted_iota(jnp.int32, (co_n, tile), 1)
        k, j = lane & (NZ - 1), (lane // NZ) & (NY - 1)
        cols = f_ref[:, at * tile:(at + 1) * tile]
        for a in range(3):
            prod = jnp.dot(w_ref[a * 9 * co_n:(a + 1) * 9 * co_n, :], cols, preferred_element_type=jnp.float32)
            total = None
            for b in range(3):
                z = [prod[(3 * b + c) * co_n:(3 * b + c + 1) * co_n] for c in range(3)]
                part = z[1] + jnp.where(k > 0, pltpu.roll(z[0], 1, 1), 0.0)
                part = part + jnp.where(k < NZ - 1, pltpu.roll(z[2], tile - 1, 1), 0.0)
                if b == 0:
                    part = jnp.where(j > 0, pltpu.roll(part, NZ, 1), 0.0)
                if b == 2:
                    part = jnp.where(j < NY - 1, pltpu.roll(part, tile - NZ, 1), 0.0)
                total = part if total is None else total + part
            ysum[a, :, at * tile:(at + 1) * tile] = total

    tiles = cells // tile
    early = tiles // 2
    for at in range(early):
        response_tile(at)

    load_g.wait()
    for copy in g_copies:
        copy.wait_recv()
    grad = jnp.concatenate([g_ref[n] for n in range(n_ci)], axis=1).astype(jnp.float32)

    turned = jnp.concatenate([grad] * (wide // co_n), axis=0).T.reshape(cells // NZ, NZ, wide)
    lane = lax.broadcasted_iota(jnp.int32, turned.shape, 2)
    k = lax.broadcasted_iota(jnp.int32, turned.shape, 1)
    before = jnp.where(k < NZ - 1, pltpu.roll(turned, NZ - 1, 1), 0.0)
    after = jnp.where((k > 0) & (lane < 3 * co_n), pltpu.roll(turned, 1, 1), 0.0)
    mixed = jnp.where(lane < co_n, before, jnp.where(lane < 2 * co_n, turned, after))
    mixed = mixed.reshape(planes, NY, NZ, wide)
    blank = jnp.zeros((planes, 1, NZ, wide), jnp.float32)
    shifted = (
        jnp.concatenate([mixed[:, 1:], blank], axis=1),
        mixed,
        jnp.concatenate([blank, mixed[:, :-1]], axis=1),
    )
    for b in range(3):
        base[b, PLANE:PLANE + cells, :] = shifted[b].reshape(cells, wide).astype(base.dtype)

    cols_w = min(2 * LANES, ci_n)
    group = 8
    per = cols_w // LANES

    def shares(h):
        for first in range(0, planes, group):
            total = None
            for a in range(3):
                for b in range(3):
                    start = (first + 2 - a) * PLANE
                    top = (3 * a + b) * depth
                    term = jnp.dot(
                        base[b, start:start + group * PLANE, :],
                        w_ref[top:top + wide, h * cols_w:(h + 1) * cols_w],
                        preferred_element_type=jnp.float32,
                    )
                    total = term if total is None else total + term
            for q in range(per):
                c = h * per + q
                for p in range(group):
                    acc[c, place(first + p, orders[c])] = total[
                        p * PLANE:(p + 1) * PLANE, q * LANES:(q + 1) * LANES
                    ]

    def where_at(c, s):
        spot = 0
        for n in range(s):
            spot = spot + co_bit(orders[c][n]) * (n_co >> (n + 1))
        return spot

    def halving(c, s):
        size = n_co >> (s + 1)
        bit = orders[c][s]
        return pltpu.make_async_remote_copy(
            src_ref=acc.at[c, pl.ds(where_at(c, s) + (1 - co_bit(bit)) * size, size)],
            dst_ref=recvs[s].at[c],
            send_sem=hs_sem.at[c * stages + s], recv_sem=hr_sem.at[c * stages + s],
            device_id={"co": co_partner(bit)}, device_id_type=MESH,
        )

    def begin(c, s):
        halving(c, s).start()

    def step(c, s):
        halving(c, s).wait_recv()
        size = n_co >> (s + 1)
        spot = pl.ds(where_at(c, s + 1), size)
        if s + 1 < stages:
            acc[c, spot] = acc[c, spot] + recvs[s][c]
            begin(c, s + 1)
        else:
            block = acc[c, where_at(c, s + 1)] + recvs[s][c, 0]
            ingrad_ref[c * LANES:(c + 1) * LANES, :] = block.T.astype(ingrad_ref.dtype)

    halves = ci_n // cols_w
    for h in range(halves):
        shares(h)
        for q in range(per):
            begin(h * per + q, 0)
    for c in range(chunks // 2):
        step(c, 0)

    for at in range(early, tiles):
        response_tile(at)
    for c in range(chunks // 2, chunks):
        step(c, 0)

    lane = lax.broadcasted_iota(jnp.int32, (co_n, cells), 1)
    whole = ysum[1] + jnp.where(lane >= PLANE, pltpu.roll(ysum[0], PLANE, 1), 0.0)
    whole = whole + jnp.where(lane < cells - PLANE, pltpu.roll(ysum[2], cells - PLANE, 1), 0.0)
    for n in range(n_ci):
        rpart[n] = whole[:, n * half:(n + 1) * half]
    r_copies = []
    for d in range(1, n_ci):
        copy = pltpu.make_async_remote_copy(
            src_ref=rpart.at[ci_other(d)], dst_ref=rrecv.at[d - 1],
            send_sem=rs_sem.at[d - 1], recv_sem=rr_sem.at[d - 1],
            device_id={"ci": ci_other(d)}, device_id_type=MESH,
        )
        copy.start()
        r_copies.append(copy)

    k, j = lane & (NZ - 1), (lane // NZ) & (NY - 1)
    edge = jnp.zeros((co_n, LANES), jnp.float32)
    along = (
        jnp.where(k < NZ - 1, pltpu.roll(grad, cells - 1, 1), 0.0),
        grad,
        jnp.where(k > 0, pltpu.roll(grad, 1, 1), 0.0),
    )
    for b in range(3):
        for c in range(3):
            v = along[c]
            if b == 0:
                v = jnp.where(j < NY - 1, pltpu.roll(v, cells - NZ, 1), 0.0)
            if b == 2:
                v = jnp.where(j > 0, pltpu.roll(v, NZ, 1), 0.0)
            rows = slice((3 * b + c) * co_n, (3 * b + c + 1) * co_n)
            u_mid[rows, :] = v.astype(u_mid.dtype)
            u_side[rows, :] = pltpu.roll(jnp.concatenate([v, edge], axis=1), PLANE, 1).astype(u_side.dtype)

    scale = float(cells) ** -0.5
    out_copies = []

    def weights(a):
        left = u_mid[...] if a == 1 else (u_side[:, 2 * PLANE:2 * PLANE + cells] if a == 0 else u_side[:, 0:cells])
        prod = lax.dot_general(left, f_ref[...], (((1,), (1,)), ((), ())), preferred_element_type=jnp.float32)
        rows = pl.ds(a * 9 * co_n, 9 * co_n)
        fg_ref[rows, :] = prod * scale
        copy = pltpu.make_async_copy(fg_ref.at[rows], fg_hbm.at[rows], out_sem.at[a])
        copy.start()
        out_copies.append(copy)

    todo = [(c, s) for t in range(1, stages + chunks) for c in range(chunks) for s in [t - c] if 1 <= s < stages]
    at_todo = 0
    for a in range(3):
        for _ in range(2):
            if at_todo < len(todo):
                step(*todo[at_todo])
                at_todo += 1
        weights(a)
    for c, s in todo[at_todo:]:
        step(c, s)

    mine = rpart[ci_me]
    for d in range(1, n_ci):
        r_copies[d - 1].wait_recv()
        mine = mine + rrecv[d - 1]
    resp_ref[...] = mine.astype(resp_ref.dtype)

    for c in range(chunks):
        for s in range(stages):
            halving(c, s).wait_send()
    for copy in g_copies + r_copies:
        copy.wait_send()
    for copy in out_copies:
        copy.wait()


def body(n_co, n_ci, features, filter_bank, out_grad):
    ci_n, cells = features.shape
    co_n, half = out_grad.shape
    stages = n_co.bit_length() - 1
    chunks = ci_n // LANES
    near = tuple(range(stages))
    far = (0,) + tuple(range(2, stages)) + (1,)
    orders = tuple(far if c == 1 else near for c in range(chunks))
    wide = -(-3 * co_n // LANES) * LANES
    rows_w = 27 * co_n
    dma = pltpu.SemaphoreType.DMA
    other = max(n_ci - 1, 1)
    scratch = [
        pltpu.VMEM((ci_n, cells), jnp.bfloat16),
        pltpu.VMEM((rows_w + wide - 3 * co_n, ci_n), jnp.bfloat16),
        pltpu.VMEM((n_ci, co_n, half), jnp.bfloat16),
        pltpu.VMEM((3, cells + 2 * PLANE, wide), jnp.bfloat16),
        pltpu.VMEM((chunks, n_co, PLANE, LANES), jnp.float32),
        [pltpu.VMEM((chunks, n_co >> (s + 1), PLANE, LANES), jnp.float32) for s in range(stages)],
        pltpu.VMEM((3, co_n, cells), jnp.float32),
        pltpu.VMEM((n_ci, co_n, half), jnp.float32),
        pltpu.VMEM((other, co_n, half), jnp.float32),
        pltpu.VMEM((9 * co_n, cells), jnp.bfloat16),
        pltpu.VMEM((9 * co_n, cells + 2 * PLANE), jnp.bfloat16),
        pltpu.VMEM((rows_w, ci_n), jnp.float32),
        dma((3,)), dma((other,)), dma((other,)), dma((other,)), dma((other,)),
        dma((chunks * stages,)), dma((chunks * stages,)), dma((3,)),
    ]
    anywhere = pl.BlockSpec(memory_space=pl.ANY)
    vmem = pl.BlockSpec(memory_space=pltpu.VMEM)
    response, in_grad, filter_grad = pl.pallas_call(
        functools.partial(kernel, n_co, n_ci, orders),
        out_shape=(
            jax.ShapeDtypeStruct((co_n, half), jnp.bfloat16),
            jax.ShapeDtypeStruct((ci_n, cells // n_co), jnp.bfloat16),
            jax.ShapeDtypeStruct((rows_w, ci_n), jnp.float32),
        ),
        in_specs=[anywhere] * 3,
        out_specs=(vmem, vmem, anywhere),
        scratch_shapes=scratch,
        compiler_params=pltpu.CompilerParams(
            collective_id=0, has_side_effects=True, vmem_limit_bytes=48 * 1024 * 1024
        ),
        cost_estimate=pl.CostEstimate(
            flops=6 * rows_w * ci_n * cells, bytes_accessed=8 * rows_w * ci_n, transcendentals=0
        ),
    )(features, filter_bank.reshape(rows_w, ci_n), out_grad)
    return response, in_grad, filter_grad.reshape(27, co_n, ci_n)


def solution(mesh):
    placed = (P("ci", None), P(None, "co", "ci"), P("co", "ci"))
    return jax.shard_map(
        functools.partial(body, mesh.shape["co"], mesh.shape["ci"]),
        mesh=mesh,
        in_specs=placed,
        out_specs=(P("co", "ci"), P("ci", "co"), P(None, "co", "ci")),
        check_vma=False,
    )
```

time: 125 us -> 47.3 us (0.38)
  matrix products: 62.4 us -> 0 us
  Pallas kernels: 0 us -> 37.1 us
  waiting for transfers between devices: 33.4 us -> 0 us
  between operations: 14.1 us -> 0.65 us
  blocking collectives: 7.27 us -> 0 us
  local copies, waits for them, and re-layouts: 4.36 us -> 9.27 us
  other arithmetic: 3.09 us -> 0 us
    conv_general_dilated x3 -> x0, matrix products: 62.4 us -> none  [the longest x1 28.4 us: body(): lax.conv_general_dilated(features.reshape(chan_in, 1, planes, NY, NZ), gr...]
    pallas_call x0 -> x1, Pallas kernels: none -> 37.1 us  [body(): pl.pallas_call(functools.partial(kernel, n_co, n_ci, orders), out_shape=(...]
    reduce_scatter x2 -> x0, waiting for transfers between devices: 33.3 us -> none  [the longest x1 33.3 us: body(): lax.psum_scatter(grad_terms, 'co', scatter_dimension=1, tiled=True)]
    all_gather x1 -> x0, blocking collectives: 7.27 us -> none  [body(): grad_full = lax.all_gather(out_grad, 'ci', axis=1, tiled=True)]
    unnamed x7 -> x9, local copies, waits for them, and re-layouts: 3.45 us -> 9.27 us
    convert_element_type x2 -> x0, other arithmetic: 3.09 us -> none  [the longest x1 1.55 us: body(): lax.psum_scatter(partial_value, 'ci', scatter_dimension=1, tiled=True)]
  transfers between devices with their start and end apart: 2 -> 0, of which waited for: 1 -> 0; matrix products, arithmetic and copies ran while one was open for 36% -> 0% of each run, Pallas kernels for 0% -> 0%
where the time goes in v1:
time: 47.3 us; the launch traced here: 47 us
  Pallas kernels  37.1 us (78%)
  local copies, waits for them, and re-layouts  9.27 us (20%)
  between operations  0.65 us (1%)
    pallas_call x1, Pallas kernels, body(): pl.pallas_call(functools.partial(kernel, n_co, n_ci, orders), out_shape=(...  37.1 us
    unnamed x9, local copies, waits for them, and re-layouts  9.27 us

profile of v1, /device:TPU:0, one launch (start us, length us, event | category | flops | bytes accessed | tf_op | source)
XLA Modules:
  0.0 47.0 jit_solution(6899792557071623403)
XLA Ops:
  0.6 0.0 copy-start
  0.6 1.5 %copy-done = bf16[27,64,512]{2,1,0:T(8,128)(2,1)S(1)} copy-done((bf16[27,64,512]{2,1,0:T(8,128)(2,1)S(1)}, bf16[27,64,512]{2,1,0:T(8,128)(2,1)}, u32[]{:S(2)}) %copy-start) | copy-done | bytes 1769496
  2.1 0.0 copy-start.1
  2.1 1.2 %copy-done.1 = bf16[512,1024]{1,0:T(8,128)(2,1)S(1)} copy-done((bf16[512,1024]{1,0:T(8,128)(2,1)S(1)}, bf16[512,1024]{1,0:T(8,128)(2,1)}, u32[]{:S(2)}) %copy-start.1) | copy-done | bytes 1048600
  3.3 0.0 copy-start.2
  3.3 0.8 %copy-done.2 = bf16[64,512]{1,0:T(8,128)(2,1)S(1)} copy-done((bf16[64,512]{1,0:T(8,128)(2,1)S(1)}, bf16[64,512]{1,0:T(8,128)(2,1)}, u32[]{:S(2)}) %copy-start.2) | copy-done | bytes 65560
  4.2 37.1 %shard_map.58 = (bf16[64,512]{1,0:T(8,128)(2,1)S(1)}, bf16[512,64]{1,0:T(8,128)(2,1)S(1)}, f32[1728,512]{1,0:T(8,128)}) custom-call(bf16[512,1024]{1,0:T(8,128)(2,1)S(1)} %copy-done.1, bf16[1728,512]{1,0:T(8,128)(2,1)S(1)} %bitcast.2, bf16[64,512]{1,0:T(8,128)(2,1)S(1)} %copy-done.2), custom_call_target="tpu_custom_call" | custom-call | flops 5435817984 | bytes 7077888 | tf_op jit(solution)/shard_map/pallas_call | solution.py:296
  41.3 0.7 %copy.6 = bf16[512,64]{0,1:T(8,128)(2,1)} copy(bf16[512,64]{1,0:T(8,128)(2,1)S(1)} %get-tuple-element.10) | data formatting | bytes 131072
  42.0 0.6 %copy.9 = bf16[64,512]{1,0:T(8,128)(2,1)} copy(bf16[64,512]{1,0:T(8,128)(2,1)S(1)} %get-tuple-element.15) | data formatting | bytes 131072
  42.7 4.4 %copy.10 = f32[27,64,512]{2,1,0:T(8,128)} copy(f32[27,64,512]{2,1,0:T(8,128)} %bitcast.3) | data formatting | bytes 7077888
Async XLA Ops:
  0.6 1.5 %copy-start = (bf16[27,64,512]{2,1,0:T(8,128)(2,1)S(1)}, bf16[27,64,512]{2,1,0:T(8,128)(2,1)}, u32[]{:S(2)}) copy-start(bf16[27,64,512]{2,1,0:T(8,128)(2,1)} %param.4) | copy-start | bytes 5308420
  2.1 1.2 %copy-start.1 = (bf16[512,1024]{1,0:T(8,128)(2,1)S(1)}, bf16[512,1024]{1,0:T(8,128)(2,1)}, u32[]{:S(2)}) copy-start(bf16[512,1024]{1,0:T(8,128)(2,1)} %f_hbm.1) | copy-start | bytes 3145732
  3.3 0.8 %copy-start.2 = (bf16[64,512]{1,0:T(8,128)(2,1)S(1)}, bf16[64,512]{1,0:T(8,128)(2,1)}, u32[]{:S(2)}) copy-start(bf16[64,512]{1,0:T(8,128)(2,1)} %g_hbm.1) | copy-start | bytes 196612

commit v2 on v1

--- a/solution.py
+++ b/solution.py
@@ -24,9 +24,9 @@
 def kernel(
     n_co, n_ci, orders,
     f_hbm, w_hbm, g_hbm,
-    resp_ref, ingrad_ref, fg_hbm,
-    f_ref, w_ref, g_ref, base, acc, recvs, ysum, rpart, rrecv, u_mid, u_side, fg_ref,
-    in_sem, gs_sem, gr_sem, rs_sem, rr_sem, hs_sem, hr_sem, out_sem,
+    resp_ref, ingrad_ref, fg_ref,
+    f_ref, w_ref, g_ref, base, acc, recvs, ysum, rpart, rrecv, u_mid, u_side,
+    in_sem, gs_sem, gr_sem, rs_sem, rr_sem, hs_sem, hr_sem,
 ):
     cells = f_ref.shape[1]
     ci_n = f_ref.shape[0]
@@ -177,7 +177,7 @@
             begin(c, s + 1)
         else:
             block = acc[c, where_at(c, s + 1)] + recvs[s][c, 0]
-            ingrad_ref[c * LANES:(c + 1) * LANES, :] = block.T.astype(ingrad_ref.dtype)
+            ingrad_ref[:, c * LANES:(c + 1) * LANES] = block.astype(ingrad_ref.dtype)
 
     halves = ci_n // cols_w
     for h in range(halves):
@@ -186,11 +186,11 @@
             begin(h * per + q, 0)
     for c in range(chunks // 2):
         step(c, 0)
-
-    for at in range(early, tiles):
-        response_tile(at)
+    response_tile(early)
     for c in range(chunks // 2, chunks):
         step(c, 0)
+    for at in range(early + 1, tiles):
+        response_tile(at)
 
     lane = lax.broadcasted_iota(jnp.int32, (co_n, cells), 1)
     whole = ysum[1] + jnp.where(lane >= PLANE, pltpu.roll(ysum[0], PLANE, 1), 0.0)
@@ -207,6 +207,13 @@
         copy.start()
         r_copies.append(copy)
 
+    todo = [(t - s, s) for t in range(1, stages + chunks) for s in range(stages - 1, 0, -1) if 0 <= t - s < chunks]
+
+    def steps(count):
+        for _ in range(min(count, len(todo))):
+            step(*todo.pop(0))
+
+    steps(1)
     k, j = lane & (NZ - 1), (lane // NZ) & (NY - 1)
     edge = jnp.zeros((co_n, LANES), jnp.float32)
     along = (
@@ -225,28 +232,21 @@
             u_mid[rows, :] = v.astype(u_mid.dtype)
             u_side[rows, :] = pltpu.roll(jnp.concatenate([v, edge], axis=1), PLANE, 1).astype(u_side.dtype)
 
+
     scale = float(cells) ** -0.5
-    out_copies = []
 
     def weights(a):
         left = u_mid[...] if a == 1 else (u_side[:, 2 * PLANE:2 * PLANE + cells] if a == 0 else u_side[:, 0:cells])
         prod = lax.dot_general(left, f_ref[...], (((1,), (1,)), ((), ())), preferred_element_type=jnp.float32)
-        rows = pl.ds(a * 9 * co_n, 9 * co_n)
-        fg_ref[rows, :] = prod * scale
-        copy = pltpu.make_async_copy(fg_ref.at[rows], fg_hbm.at[rows], out_sem.at[a])
-        copy.start()
-        out_copies.append(copy)
-
-    todo = [(c, s) for t in range(1, stages + chunks) for c in range(chunks) for s in [t - c] if 1 <= s < stages]
-    at_todo = 0
-    for a in range(3):
-        for _ in range(2):
-            if at_todo < len(todo):
-                step(*todo[at_todo])
-                at_todo += 1
-        weights(a)
-    for c, s in todo[at_todo:]:
-        step(c, s)
+        fg_ref[a * 9 * co_n:(a + 1) * 9 * co_n, :] = prod * scale
+
+    steps(2)
+    weights(1)
+    steps(3)
+    weights(0)
+    steps(3)
+    weights(2)
+    steps(len(todo))
 
     mine = rpart[ci_me]
     for d in range(1, n_ci):
@@ -259,7 +259,17 @@
             halving(c, s).wait_send()
     for copy in g_copies + r_copies:
         copy.wait_send()
-    for copy in out_copies:
+
+
+def hand_over(r_ref, i_ref, w_ref, r_out, i_out, w_out, sem):
+    rows = w_ref.shape[0] // 3
+    copies = [pltpu.make_async_copy(r_ref, r_out, sem.at[0]), pltpu.make_async_copy(i_ref, i_out, sem.at[1])]
+    for a in range(3):
+        part = pl.ds(a * rows, rows)
+        copies.append(pltpu.make_async_copy(w_ref.at[part], w_out.at[part], sem.at[2 + a]))
+    for copy in copies:
+        copy.start()
+    for copy in copies:
         copy.wait()
 
 
@@ -287,30 +297,38 @@
         pltpu.VMEM((other, co_n, half), jnp.float32),
         pltpu.VMEM((9 * co_n, cells), jnp.bfloat16),
         pltpu.VMEM((9 * co_n, cells + 2 * PLANE), jnp.bfloat16),
-        pltpu.VMEM((rows_w, ci_n), jnp.float32),
         dma((3,)), dma((other,)), dma((other,)), dma((other,)), dma((other,)),
-        dma((chunks * stages,)), dma((chunks * stages,)), dma((3,)),
+        dma((chunks * stages,)), dma((chunks * stages,)),
     ]
-    anywhere = pl.BlockSpec(memory_space=pl.ANY)
+    hbm = pl.BlockSpec(memory_space=pltpu.HBM)
     vmem = pl.BlockSpec(memory_space=pltpu.VMEM)
-    response, in_grad, filter_grad = pl.pallas_call(
+    shapes = (
+        jax.ShapeDtypeStruct((co_n, half), jnp.bfloat16),
+        jax.ShapeDtypeStruct((cells // n_co, ci_n), jnp.bfloat16),
+        jax.ShapeDtypeStruct((rows_w, ci_n), jnp.float32),
+    )
+    results = pl.pallas_call(
         functools.partial(kernel, n_co, n_ci, orders),
-        out_shape=(
-            jax.ShapeDtypeStruct((co_n, half), jnp.bfloat16),
-            jax.ShapeDtypeStruct((ci_n, cells // n_co), jnp.bfloat16),
-            jax.ShapeDtypeStruct((rows_w, ci_n), jnp.float32),
-        ),
-        in_specs=[anywhere] * 3,
-        out_specs=(vmem, vmem, anywhere),
+        out_shape=shapes,
+        in_specs=[hbm] * 3,
+        out_specs=(vmem,) * 3,
         scratch_shapes=scratch,
         compiler_params=pltpu.CompilerParams(
-            collective_id=0, has_side_effects=True, vmem_limit_bytes=48 * 1024 * 1024
+            collective_id=0, has_side_effects=True, vmem_limit_bytes=32 * 1024 * 1024
         ),
         cost_estimate=pl.CostEstimate(
             flops=6 * rows_w * ci_n * cells, bytes_accessed=8 * rows_w * ci_n, transcendentals=0
         ),
-    )(features, filter_bank.reshape(rows_w, ci_n), out_grad)
-    return response, in_grad, filter_grad.reshape(27, co_n, ci_n)
+    )(*[pltpu.with_memory_space_constraint(v, pltpu.HBM) for v in (features, filter_bank.reshape(rows_w, ci_n), out_grad)])
+    response, in_grad, filter_grad = pl.pallas_call(
+        hand_over,
+        out_shape=shapes,
+        in_specs=[vmem] * 3,
+        out_specs=(hbm,) * 3,
+        scratch_shapes=[dma((5,))],
+        cost_estimate=pl.CostEstimate(flops=0, bytes_accessed=8 * rows_w * ci_n, transcendentals=0),
+    )(*results)
+    return response, in_grad.T, filter_grad.reshape(27, co_n, ci_n)
 
 
 def solution(mesh):

time: 47.3 us -> 43.6 us (0.922)
  local copies, waits for them, and re-layouts: 9.27 us -> 2.99 us
  Pallas kernels: 37.1 us -> 39.8 us
    unnamed x9 -> x6, local copies, waits for them, and re-layouts: 9.27 us -> 2.99 us
    pallas_call x1 -> x2, Pallas kernels: 37.1 us -> 39.8 us  [the longest x1 35.8 us: body(): pl.pallas_call(functools.partial(kernel, n_co, n_ci, orders), out_shape=s...]
where the time goes in v2:
time: 43.6 us; the launch traced here: 43.4 us
  Pallas kernels  39.8 us (91%)
  local copies, waits for them, and re-layouts  2.99 us (7%)
  between operations  0.65 us (1%)
    pallas_call x1, Pallas kernels, body(): pl.pallas_call(functools.partial(kernel, n_co, n_ci, orders), out_shape=s...  35.8 us
    pallas_call x1, Pallas kernels, body(): pl.pallas_call(hand_over, out_shape=shapes, in_specs=[vmem] * 3, out_spec...  3.95 us
    unnamed x6, local copies, waits for them, and re-layouts  2.99 us

profile of v2, /device:TPU:0, one launch (start us, length us, event | category | flops | bytes accessed | tf_op | source)
XLA Modules:
  0.0 43.4 jit_solution(2000108067780500014)
XLA Ops:
  0.6 35.8 %shard_map.58 = (bf16[64,512]{1,0:T(8,128)(2,1)S(1)}, bf16[64,512]{1,0:T(8,128)(2,1)S(1)}, f32[1728,512]{1,0:T(8,128)S(1)}) custom-call(bf16[512,1024]{1,0:T(8,128)(2,1)} %f_hbm.1, bf16[1728,512]{1,0:T(8,128)(2,1)} %bitcast.4, bf16[64,512]{1,0:T(8,128)(2,1)} %g_hbm.1), custom_call_target="tpu_custom_call" | custom-call | flops 5435817984 | bytes 7077888 | tf_op jit(solution)/shard_map/pallas_call | solution.py:310
  36.5 0.0 copy-start
  36.5 1.7 %copy-done = f32[1728,512]{1,0:T(8,128)} copy-done((f32[1728,512]{1,0:T(8,128)}, f32[1728,512]{1,0:T(8,128)S(1)}, u32[]{:S(2)}) %copy-start) | copy-done | bytes 3538968
  38.2 0.0 copy-start.1
  38.2 0.6 %copy-done.1 = bf16[64,512]{1,0:T(8,128)(2,1)} copy-done((bf16[64,512]{1,0:T(8,128)(2,1)}, bf16[64,512]{1,0:T(8,128)(2,1)S(1)}, u32[]{:S(2)}) %copy-start.1) | copy-done | bytes 65560
  38.8 0.0 copy-start.2
  38.8 0.6 %copy-done.2 = bf16[64,512]{1,0:T(8,128)(2,1)} copy-done((bf16[64,512]{1,0:T(8,128)(2,1)}, bf16[64,512]{1,0:T(8,128)(2,1)S(1)}, u32[]{:S(2)}) %copy-start.2) | copy-done | bytes 65560
  39.5 4.0 %shard_map.59 = (bf16[64,512]{1,0:T(8,128)(2,1)}, bf16[64,512]{1,0:T(8,128)(2,1)}, f32[1728,512]{1,0:T(8,128)}) custom-call(bf16[64,512]{1,0:T(8,128)(2,1)} %copy-done.1, bf16[64,512]{1,0:T(8,128)(2,1)} %copy-done.2, f32[1728,512]{1,0:T(8,128)} %copy-done), custom_call_target="tpu_custom_call" | custom-call | bytes 7077888 | tf_op jit(solution)/shard_map/pallas_call | solution.py:323
Async XLA Ops:
  36.5 1.8 %copy-start = (f32[1728,512]{1,0:T(8,128)}, f32[1728,512]{1,0:T(8,128)S(1)}, u32[]{:S(2)}) copy-start(f32[1728,512]{1,0:T(8,128)S(1)} %get-tuple-element.11.w_ref) | copy-start | bytes 10616836
  38.2 0.6 %copy-start.1 = (bf16[64,512]{1,0:T(8,128)(2,1)}, bf16[64,512]{1,0:T(8,128)(2,1)S(1)}, u32[]{:S(2)}) copy-start(bf16[64,512]{1,0:T(8,128)(2,1)S(1)} %get-tuple-element.9.r_ref) | copy-start | bytes 196612
  38.8 0.6 %copy-start.2 = (bf16[64,512]{1,0:T(8,128)(2,1)}, bf16[64,512]{1,0:T(8,128)(2,1)S(1)}, u32[]{:S(2)}) copy-start(bf16[64,512]{1,0:T(8,128)(2,1)S(1)} %get-tuple-element.10.i_ref) | copy-start | bytes 196612

commit v3 on v2

--- a/solution.py
+++ b/solution.py
@@ -168,29 +168,34 @@
     def begin(c, s):
         halving(c, s).start()
 
-    def step(c, s):
+    def arrive(c, s):
         halving(c, s).wait_recv()
         size = n_co >> (s + 1)
         spot = pl.ds(where_at(c, s + 1), size)
         if s + 1 < stages:
             acc[c, spot] = acc[c, spot] + recvs[s][c]
-            begin(c, s + 1)
         else:
             block = acc[c, where_at(c, s + 1)] + recvs[s][c, 0]
             ingrad_ref[:, c * LANES:(c + 1) * LANES] = block.astype(ingrad_ref.dtype)
+
+    def step(c, s):
+        arrive(c, s)
+        if s + 1 < stages:
+            begin(c, s + 1)
 
     halves = ci_n // cols_w
     for h in range(halves):
         shares(h)
         for q in range(per):
             begin(h * per + q, 0)
-    for c in range(chunks // 2):
-        step(c, 0)
-    response_tile(early)
-    for c in range(chunks // 2, chunks):
-        step(c, 0)
-    for at in range(early + 1, tiles):
+    lead = [0] + list(range(2, chunks))
+    step(0, 0)
+    if chunks > 1:
+        step(1, 0)
+    for at in range(early, tiles):
         response_tile(at)
+    for c in lead[1:]:
+        arrive(c, 0)
 
     lane = lax.broadcasted_iota(jnp.int32, (co_n, cells), 1)
     whole = ysum[1] + jnp.where(lane >= PLANE, pltpu.roll(ysum[0], PLANE, 1), 0.0)
@@ -207,13 +212,6 @@
         copy.start()
         r_copies.append(copy)
 
-    todo = [(t - s, s) for t in range(1, stages + chunks) for s in range(stages - 1, 0, -1) if 0 <= t - s < chunks]
-
-    def steps(count):
-        for _ in range(min(count, len(todo))):
-            step(*todo.pop(0))
-
-    steps(1)
     k, j = lane & (NZ - 1), (lane // NZ) & (NY - 1)
     edge = jnp.zeros((co_n, LANES), jnp.float32)
     along = (
@@ -221,7 +219,8 @@
         grad,
         jnp.where(k > 0, pltpu.roll(grad, 1, 1), 0.0),
     )
-    for b in range(3):
+
+    def lay(b):
         for c in range(3):
             v = along[c]
             if b == 0:
@@ -232,21 +231,41 @@
             u_mid[rows, :] = v.astype(u_mid.dtype)
             u_side[rows, :] = pltpu.roll(jnp.concatenate([v, edge], axis=1), PLANE, 1).astype(u_side.dtype)
 
-
     scale = float(cells) ** -0.5
 
-    def weights(a):
+    def weights(a, h):
         left = u_mid[...] if a == 1 else (u_side[:, 2 * PLANE:2 * PLANE + cells] if a == 0 else u_side[:, 0:cells])
-        prod = lax.dot_general(left, f_ref[...], (((1,), (1,)), ((), ())), preferred_element_type=jnp.float32)
-        fg_ref[a * 9 * co_n:(a + 1) * 9 * co_n, :] = prod * scale
-
-    steps(2)
-    weights(1)
-    steps(3)
-    weights(0)
-    steps(3)
-    weights(2)
-    steps(len(todo))
+        cols = slice(h * cols_w, (h + 1) * cols_w)
+        prod = lax.dot_general(left, f_ref[cols, :], (((1,), (1,)), ((), ())), preferred_element_type=jnp.float32)
+        fg_ref[a * 9 * co_n:(a + 1) * 9 * co_n, cols] = prod * scale
+
+    work = [functools.partial(lay, b) for b in range(3)]
+    work += [functools.partial(weights, a, h) for a in range(3) for h in range(halves)]
+
+    def compute(count):
+        for _ in range(min(count, len(work))):
+            work.pop(0)()
+
+    compute(1)
+    open_at = {1: 1} if chunks > 1 else {}
+    for turn, c in enumerate(lead):
+        step(c, 1)
+        if turn + 1 < len(lead):
+            begin(lead[turn + 1], 1)
+        for other in list(open_at):
+            if open_at[other] < stages:
+                step(other, open_at[other])
+                open_at[other] += 1
+            compute(1)
+        open_at[c] = 2
+        compute(1)
+    while any(s < stages for s in open_at.values()):
+        for other in open_at:
+            if open_at[other] < stages:
+                step(other, open_at[other])
+                open_at[other] += 1
+                compute(1)
+    compute(len(work))
 
     mine = rpart[ci_me]
     for d in range(1, n_ci):
@@ -262,11 +281,11 @@
 
 
 def hand_over(r_ref, i_ref, w_ref, r_out, i_out, w_out, sem):
-    rows = w_ref.shape[0] // 3
+    rows = w_ref.shape[0] // 27
     copies = [pltpu.make_async_copy(r_ref, r_out, sem.at[0]), pltpu.make_async_copy(i_ref, i_out, sem.at[1])]
-    for a in range(3):
-        part = pl.ds(a * rows, rows)
-        copies.append(pltpu.make_async_copy(w_ref.at[part], w_out.at[part], sem.at[2 + a]))
+    for t in range(27):
+        part = pl.ds(t * rows, rows)
+        copies.append(pltpu.make_async_copy(w_ref.at[part], w_out.at[part], sem.at[2 + t]))
     for copy in copies:
         copy.start()
     for copy in copies:
@@ -325,9 +344,10 @@
         out_shape=shapes,
         in_specs=[vmem] * 3,
         out_specs=(hbm,) * 3,
-        scratch_shapes=[dma((5,))],
+        scratch_shapes=[dma((29,))],
+        compiler_params=pltpu.CompilerParams(vmem_limit_bytes=8 * 1024 * 1024),
         cost_estimate=pl.CostEstimate(flops=0, bytes_accessed=8 * rows_w * ci_n, transcendentals=0),
-    )(*results)
+    )(*[pltpu.with_memory_space_constraint(v, pltpu.VMEM) for v in results])
     return response, in_grad.T, filter_grad.reshape(27, co_n, ci_n)
 
 

time: 43.6 us -> 36.6 us (0.84)
  Pallas kernels: 39.8 us -> 35.8 us
  local copies, waits for them, and re-layouts: 2.99 us -> 0 us
    unnamed x6 -> x0, local copies, waits for them, and re-layouts: 2.99 us -> none
    pallas_call x1, Pallas kernels: 35.8 us -> 33.7 us  [body(): pl.pallas_call(functools.partial(kernel, n_co, n_ci, orders), out_shape=s...]
    pallas_call x1, Pallas kernels: 3.95 us -> 2.07 us  [body(): pl.pallas_call(hand_over, out_shape=shapes, in_specs=[vmem] * 3, out_spec...]
where the time goes in v3:
time: 36.6 us; the launch traced here: 36.5 us
  Pallas kernels  35.8 us (98%)
  between operations  0.64 us (2%)
    pallas_call x1, Pallas kernels, body(): pl.pallas_call(functools.partial(kernel, n_co, n_ci, orders), out_shape=s...  33.7 us
    pallas_call x1, Pallas kernels, body(): pl.pallas_call(hand_over, out_shape=shapes, in_specs=[vmem] * 3, out_spec...  2.07 us

profile of v3, /device:TPU:0, one launch (start us, length us, event | category | flops | bytes accessed | tf_op | source)
XLA Modules:
  0.0 36.5 jit_solution(1990251423104780109)
XLA Ops:
  0.6 33.7 %shard_map.58 = (bf16[64,512]{1,0:T(8,128)(2,1)S(1)}, bf16[64,512]{1,0:T(8,128)(2,1)S(1)}, f32[1728,512]{1,0:T(8,128)S(1)}) custom-call(bf16[512,1024]{1,0:T(8,128)(2,1)} %f_hbm.1, bf16[1728,512]{1,0:T(8,128)(2,1)} %bitcast.4, bf16[64,512]{1,0:T(8,128)(2,1)} %g_hbm.1), custom_call_target="tpu_custom_call" | custom-call | flops 5435817984 | bytes 7077888 | tf_op jit(solution)/shard_map/pallas_call | solution.py:329
  34.4 2.1 %shard_map.59 = (bf16[64,512]{1,0:T(8,128)(2,1)}, bf16[64,512]{1,0:T(8,128)(2,1)}, f32[1728,512]{1,0:T(8,128)}) custom-call(bf16[64,512]{1,0:T(8,128)(2,1)S(1)} %get-tuple-element.9.r_ref, bf16[64,512]{1,0:T(8,128)(2,1)S(1)} %get-tuple-element.10.i_ref, f32[1728,512]{1,0:T(8,128)S(1)} %get-tuple-element.11.w_ref), custom_call_target="tpu_custom_call" | custom-call | bytes 7077888 | tf_op jit(solution)/shard_map/pallas_call | solution.py:342

commit v4 on v3

--- a/solution.py
+++ b/solution.py
@@ -76,6 +76,30 @@
     w_ref[rows_w:, :] = jnp.zeros((w_ref.shape[0] - rows_w, ci_n), w_ref.dtype)
     base[:, 0:PLANE, :] = jnp.zeros((3, PLANE, wide), base.dtype)
     base[:, PLANE + cells:, :] = jnp.zeros((3, PLANE, wide), base.dtype)
+    def rows_of(owner):
+        lane = lax.broadcasted_iota(jnp.int32, (LANES // NZ, NZ, wide), 2)
+        k = lax.broadcasted_iota(jnp.int32, (LANES // NZ, NZ, wide), 1)
+        first, last = (lane < co_n) & (k < NZ - 1), (lane >= 2 * co_n) & (lane < 3 * co_n) & (k > 0)
+        middle = (lane >= co_n) & (lane < 2 * co_n)
+        blank = jnp.zeros((LANES // PLANE, 1, NZ, wide), jnp.float32)
+        for at in range(half // LANES):
+            block = g_ref[owner, :, at * LANES:(at + 1) * LANES].astype(jnp.float32)
+            turned = jnp.concatenate([block] * (wide // co_n), axis=0).T.reshape(LANES // NZ, NZ, wide)
+            mixed = jnp.where(middle, turned, 0.0)
+            mixed = jnp.where(first, pltpu.roll(turned, NZ - 1, 1), mixed)
+            mixed = jnp.where(last, pltpu.roll(turned, 1, 1), mixed)
+            mixed = mixed.reshape(LANES // PLANE, NY, NZ, wide)
+            shifted = (
+                jnp.concatenate([mixed[:, 1:], blank], axis=1),
+                mixed,
+                jnp.concatenate([blank, mixed[:, :-1]], axis=1),
+            )
+            rows = pl.ds(pl.multiple_of(PLANE + owner * half + at * LANES, PLANE), LANES)
+            for b in range(3):
+                base[b, rows, :] = shifted[b].reshape(LANES, wide).astype(base.dtype)
+
+    load_g.wait()
+    rows_of(ci_me)
     load_w.wait()
     load_f.wait()
 
@@ -104,26 +128,9 @@
     for at in range(early):
         response_tile(at)
 
-    load_g.wait()
-    for copy in g_copies:
-        copy.wait_recv()
-    grad = jnp.concatenate([g_ref[n] for n in range(n_ci)], axis=1).astype(jnp.float32)
-
-    turned = jnp.concatenate([grad] * (wide // co_n), axis=0).T.reshape(cells // NZ, NZ, wide)
-    lane = lax.broadcasted_iota(jnp.int32, turned.shape, 2)
-    k = lax.broadcasted_iota(jnp.int32, turned.shape, 1)
-    before = jnp.where(k < NZ - 1, pltpu.roll(turned, NZ - 1, 1), 0.0)
-    after = jnp.where((k > 0) & (lane < 3 * co_n), pltpu.roll(turned, 1, 1), 0.0)
-    mixed = jnp.where(lane < co_n, before, jnp.where(lane < 2 * co_n, turned, after))
-    mixed = mixed.reshape(planes, NY, NZ, wide)
-    blank = jnp.zeros((planes, 1, NZ, wide), jnp.float32)
-    shifted = (
-        jnp.concatenate([mixed[:, 1:], blank], axis=1),
-        mixed,
-        jnp.concatenate([blank, mixed[:, :-1]], axis=1),
-    )
-    for b in range(3):
-        base[b, PLANE:PLANE + cells, :] = shifted[b].reshape(cells, wide).astype(base.dtype)
+    for d in range(1, n_ci):
+        g_copies[d - 1].wait_recv()
+        rows_of(lax.rem(ci_me + n_ci - d, n_ci))
 
     cols_w = min(2 * LANES, ci_n)
     group = 8
@@ -132,16 +139,15 @@
     def shares(h):
         for first in range(0, planes, group):
             total = None
-            for a in range(3):
-                for b in range(3):
-                    start = (first + 2 - a) * PLANE
-                    top = (3 * a + b) * depth
-                    term = jnp.dot(
-                        base[b, start:start + group * PLANE, :],
-                        w_ref[top:top + wide, h * cols_w:(h + 1) * cols_w],
-                        preferred_element_type=jnp.float32,
-                    )
-                    total = term if total is None else total + term
+            for b in range(3):
+                starts = [(first + 2 - a) * PLANE for a in range(3)]
+                tops = [(3 * a + b) * depth for a in range(3)]
+                term = jnp.dot(
+                    jnp.concatenate([base[b, start:start + group * PLANE, :] for start in starts], axis=1),
+                    jnp.concatenate([w_ref[top:top + wide, h * cols_w:(h + 1) * cols_w] for top in tops], axis=0),
+                    preferred_element_type=jnp.float32,
+                )
+                total = term if total is None else total + term
             for q in range(per):
                 c = h * per + q
                 for p in range(group):
@@ -196,6 +202,8 @@
         response_tile(at)
     for c in lead[1:]:
         arrive(c, 0)
+        if c == lead[1]:
+            begin(c, 1)
 
     lane = lax.broadcasted_iota(jnp.int32, (co_n, cells), 1)
     whole = ysum[1] + jnp.where(lane >= PLANE, pltpu.roll(ysum[0], PLANE, 1), 0.0)
@@ -212,24 +220,27 @@
         copy.start()
         r_copies.append(copy)
 
+    strip = 16
+    lane = lax.broadcasted_iota(jnp.int32, (strip, cells), 1)
     k, j = lane & (NZ - 1), (lane // NZ) & (NY - 1)
-    edge = jnp.zeros((co_n, LANES), jnp.float32)
-    along = (
-        jnp.where(k < NZ - 1, pltpu.roll(grad, cells - 1, 1), 0.0),
-        grad,
-        jnp.where(k > 0, pltpu.roll(grad, 1, 1), 0.0),
-    )
-
-    def lay(b):
-        for c in range(3):
-            v = along[c]
-            if b == 0:
-                v = jnp.where(j < NY - 1, pltpu.roll(v, cells - NZ, 1), 0.0)
-            if b == 2:
-                v = jnp.where(j > 0, pltpu.roll(v, NZ, 1), 0.0)
-            rows = slice((3 * b + c) * co_n, (3 * b + c + 1) * co_n)
-            u_mid[rows, :] = v.astype(u_mid.dtype)
-            u_side[rows, :] = pltpu.roll(jnp.concatenate([v, edge], axis=1), PLANE, 1).astype(u_side.dtype)
+    edge = jnp.zeros((strip, LANES), jnp.float32)
+
+    def lay(c):
+        for top in range(0, co_n, strip):
+            v = jnp.concatenate([g_ref[n, top:top + strip, :] for n in range(n_ci)], axis=1).astype(jnp.float32)
+            if c == 0:
+                v = jnp.where(k < NZ - 1, pltpu.roll(v, cells - 1, 1), 0.0)
+            if c == 2:
+                v = jnp.where(k > 0, pltpu.roll(v, 1, 1), 0.0)
+            for b in range(3):
+                u = v
+                if b == 0:
+                    u = jnp.where(j < NY - 1, pltpu.roll(v, cells - NZ, 1), 0.0)
+                if b == 2:
+                    u = jnp.where(j > 0, pltpu.roll(v, NZ, 1), 0.0)
+                rows = slice((3 * b + c) * co_n + top, (3 * b + c) * co_n + top + strip)
+                u_mid[rows, :] = u.astype(u_mid.dtype)
+                u_side[rows, :] = pltpu.roll(jnp.concatenate([u, edge], axis=1), PLANE, 1).astype(u_side.dtype)
 
     scale = float(cells) ** -0.5
 
@@ -239,7 +250,7 @@
         prod = lax.dot_general(left, f_ref[cols, :], (((1,), (1,)), ((), ())), preferred_element_type=jnp.float32)
         fg_ref[a * 9 * co_n:(a + 1) * 9 * co_n, cols] = prod * scale
 
-    work = [functools.partial(lay, b) for b in range(3)]
+    work = [functools.partial(lay, c) for c in range(3)]
     work += [functools.partial(weights, a, h) for a in range(3) for h in range(halves)]
 
     def compute(count):
@@ -250,8 +261,8 @@
     open_at = {1: 1} if chunks > 1 else {}
     for turn, c in enumerate(lead):
         step(c, 1)
-        if turn + 1 < len(lead):
-            begin(lead[turn + 1], 1)
+        if turn + 2 < len(lead):
+            begin(lead[turn + 2], 1)
         for other in list(open_at):
             if open_at[other] < stages:
                 step(other, open_at[other])

time: 36.6 us -> 36.3 us (level)
  no operation moved by 1% of the time
where the time goes in v4:
time: 36.3 us; the launch traced here: 36.1 us
  Pallas kernels  35.5 us (98%)
  between operations  0.64 us (2%)
    pallas_call x1, Pallas kernels, body(): pl.pallas_call(functools.partial(kernel, n_co, n_ci, orders), out_shape=s...  33.4 us
    pallas_call x1, Pallas kernels, body(): pl.pallas_call(hand_over, out_shape=shapes, in_specs=[vmem] * 3, out_spec...  2.07 us

profile of v4, /device:TPU:0, one launch (start us, length us, event | category | flops | bytes accessed | tf_op | source)
XLA Modules:
  0.0 36.1 jit_solution(2365134000598160318)
XLA Ops:
  0.6 33.4 %shard_map.58 = (bf16[64,512]{1,0:T(8,128)(2,1)S(1)}, bf16[64,512]{1,0:T(8,128)(2,1)S(1)}, f32[1728,512]{1,0:T(8,128)S(1)}) custom-call(bf16[512,1024]{1,0:T(8,128)(2,1)} %f_hbm.1, bf16[1728,512]{1,0:T(8,128)(2,1)} %bitcast.4, bf16[64,512]{1,0:T(8,128)(2,1)} %g_hbm.1), custom_call_target="tpu_custom_call" | custom-call | flops 5435817984 | bytes 7077888 | tf_op jit(solution)/shard_map/pallas_call | solution.py:340
  34.0 2.1 %shard_map.59 = (bf16[64,512]{1,0:T(8,128)(2,1)}, bf16[64,512]{1,0:T(8,128)(2,1)}, f32[1728,512]{1,0:T(8,128)}) custom-call(bf16[64,512]{1,0:T(8,128)(2,1)S(1)} %get-tuple-element.9.r_ref, bf16[64,512]{1,0:T(8,128)(2,1)S(1)} %get-tuple-element.10.i_ref, f32[1728,512]{1,0:T(8,128)S(1)} %get-tuple-element.11.w_ref), custom_call_target="tpu_custom_call" | custom-call | bytes 7077888 | tf_op jit(solution)/shard_map/pallas_call | solution.py:353

commit v5 on v4

--- a/solution.py
+++ b/solution.py
@@ -37,6 +37,8 @@
     wide = base.shape[2]
     stages = len(orders[0])
     chunks = len(orders)
+    part = acc.shape[2]
+    pieces = PLANE // part
     co_me = lax.axis_index("co")
     ci_me = lax.axis_index("ci")
 
@@ -124,9 +126,6 @@
             ysum[a, :, at * tile:(at + 1) * tile] = total
 
     tiles = cells // tile
-    early = tiles // 2
-    for at in range(early):
-        response_tile(at)
 
     for d in range(1, n_ci):
         g_copies[d - 1].wait_recv()
@@ -149,11 +148,11 @@
                 )
                 total = term if total is None else total + term
             for q in range(per):
-                c = h * per + q
-                for p in range(group):
-                    acc[c, place(first + p, orders[c])] = total[
-                        p * PLANE:(p + 1) * PLANE, q * LANES:(q + 1) * LANES
-                    ]
+                for r in range(pieces):
+                    c = (h * per + q) * pieces + r
+                    for p in range(group):
+                        top = p * PLANE + r * part
+                        acc[c, place(first + p, orders[c])] = total[top:top + part, q * LANES:(q + 1) * LANES]
 
     def where_at(c, s):
         spot = 0
@@ -182,7 +181,8 @@
             acc[c, spot] = acc[c, spot] + recvs[s][c]
         else:
             block = acc[c, where_at(c, s + 1)] + recvs[s][c, 0]
-            ingrad_ref[:, c * LANES:(c + 1) * LANES] = block.astype(ingrad_ref.dtype)
+            q, r = c // pieces, c % pieces
+            ingrad_ref[r * part:(r + 1) * part, q * LANES:(q + 1) * LANES] = block.astype(ingrad_ref.dtype)
 
     def step(c, s):
         arrive(c, s)
@@ -190,20 +190,22 @@
             begin(c, s + 1)
 
     halves = ci_n // cols_w
+    lead = [c for c in range(chunks) if orders[c][1] == 1]
+    side = [c for c in range(chunks) if orders[c][1] != 1]
+    flying = 3
     for h in range(halves):
         shares(h)
-        for q in range(per):
-            begin(h * per + q, 0)
-    lead = [0] + list(range(2, chunks))
-    step(0, 0)
-    if chunks > 1:
-        step(1, 0)
-    for at in range(early, tiles):
+        for c in range(h * per * pieces, (h + 1) * per * pieces):
+            begin(c, 0)
+    for c in lead[:flying - 1] + side:
+        step(c, 0)
+    response_tile(0)
+    for c in lead[flying - 1:flying]:
+        step(c, 0)
+    for at in range(1, tiles):
         response_tile(at)
-    for c in lead[1:]:
+    for c in lead[flying:]:
         arrive(c, 0)
-        if c == lead[1]:
-            begin(c, 1)
 
     lane = lax.broadcasted_iota(jnp.int32, (co_n, cells), 1)
     whole = ysum[1] + jnp.where(lane >= PLANE, pltpu.roll(ysum[0], PLANE, 1), 0.0)
@@ -258,24 +260,24 @@
             work.pop(0)()
 
     compute(1)
-    open_at = {1: 1} if chunks > 1 else {}
+    reached = {c: 1 for c in side}
+
+    def advance():
+        for c in list(reached):
+            if reached[c] < stages:
+                step(c, reached[c])
+                reached[c] += 1
+
     for turn, c in enumerate(lead):
         step(c, 1)
-        if turn + 2 < len(lead):
-            begin(lead[turn + 2], 1)
-        for other in list(open_at):
-            if open_at[other] < stages:
-                step(other, open_at[other])
-                open_at[other] += 1
-            compute(1)
-        open_at[c] = 2
+        if turn + flying < len(lead):
+            begin(lead[turn + flying], 1)
         compute(1)
-    while any(s < stages for s in open_at.values()):
-        for other in open_at:
-            if open_at[other] < stages:
-                step(other, open_at[other])
-                open_at[other] += 1
-                compute(1)
+        advance()
+        reached[c] = 2
+        compute(1)
+    while any(s < stages for s in reached.values()):
+        advance()
     compute(len(work))
 
     mine = rpart[ci_me]
@@ -307,10 +309,11 @@
     ci_n, cells = features.shape
     co_n, half = out_grad.shape
     stages = n_co.bit_length() - 1
-    chunks = ci_n // LANES
+    pieces = 2
+    chunks = ci_n // LANES * pieces
     near = tuple(range(stages))
     far = (0,) + tuple(range(2, stages)) + (1,)
-    orders = tuple(far if c == 1 else near for c in range(chunks))
+    orders = tuple(far if c // pieces == 1 else near for c in range(chunks))
     wide = -(-3 * co_n // LANES) * LANES
     rows_w = 27 * co_n
     dma = pltpu.SemaphoreType.DMA
@@ -320,8 +323,8 @@
         pltpu.VMEM((rows_w + wide - 3 * co_n, ci_n), jnp.bfloat16),
         pltpu.VMEM((n_ci, co_n, half), jnp.bfloat16),
         pltpu.VMEM((3, cells + 2 * PLANE, wide), jnp.bfloat16),
-        pltpu.VMEM((chunks, n_co, PLANE, LANES), jnp.float32),
-        [pltpu.VMEM((chunks, n_co >> (s + 1), PLANE, LANES), jnp.float32) for s in range(stages)],
+        pltpu.VMEM((chunks, n_co, PLANE // pieces, LANES), jnp.float32),
+        [pltpu.VMEM((chunks, n_co >> (s + 1), PLANE // pieces, LANES), jnp.float32) for s in range(stages)],
         pltpu.VMEM((3, co_n, cells), jnp.float32),
         pltpu.VMEM((n_ci, co_n, half), jnp.float32),
         pltpu.VMEM((other, co_n, half), jnp.float32),

time: 36.3 us -> 43.9 us (1.21)
  Pallas kernels: 35.5 us -> 43.1 us
    pallas_call x1, Pallas kernels: 33.4 us -> 41 us  [body(): pl.pallas_call(functools.partial(kernel, n_co, n_ci, orders), out_shape=s...]
where the time goes in v5:
time: 43.9 us; the launch traced here: 43.7 us
  Pallas kernels  43.1 us (98%)
  between operations  0.64 us (1%)
    pallas_call x1, Pallas kernels, body(): pl.pallas_call(functools.partial(kernel, n_co, n_ci, orders), out_shape=s...  41 us
    pallas_call x1, Pallas kernels, body(): pl.pallas_call(hand_over, out_shape=shapes, in_specs=[vmem] * 3, out_spec...  2.07 us

profile of v5, /device:TPU:0, one launch (start us, length us, event | category | flops | bytes accessed | tf_op | source)
XLA Modules:
  0.0 43.7 jit_solution(849205077373811880)
XLA Ops:
  0.6 41.0 %shard_map.58 = (bf16[64,512]{1,0:T(8,128)(2,1)S(1)}, bf16[64,512]{1,0:T(8,128)(2,1)S(1)}, f32[1728,512]{1,0:T(8,128)S(1)}) custom-call(bf16[512,1024]{1,0:T(8,128)(2,1)} %f_hbm.1, bf16[1728,512]{1,0:T(8,128)(2,1)} %bitcast.4, bf16[64,512]{1,0:T(8,128)(2,1)} %g_hbm.1), custom_call_target="tpu_custom_call" | custom-call | flops 5435817984 | bytes 7077888 | tf_op jit(solution)/shard_map/pallas_call | solution.py:343
  41.7 2.1 %shard_map.59 = (bf16[64,512]{1,0:T(8,128)(2,1)}, bf16[64,512]{1,0:T(8,128)(2,1)}, f32[1728,512]{1,0:T(8,128)}) custom-call(bf16[64,512]{1,0:T(8,128)(2,1)S(1)} %get-tuple-element.9.r_ref, bf16[64,512]{1,0:T(8,128)(2,1)S(1)} %get-tuple-element.10.i_ref, f32[1728,512]{1,0:T(8,128)S(1)} %get-tuple-element.11.w_ref), custom_call_target="tpu_custom_call" | custom-call | bytes 7077888 | tf_op jit(solution)/shard_map/pallas_call | solution.py:356

commit v6 on v4

--- a/solution.py
+++ b/solution.py
@@ -37,6 +37,7 @@
     wide = base.shape[2]
     stages = len(orders[0])
     chunks = len(orders)
+    cut = acc.shape[3]
     co_me = lax.axis_index("co")
     ci_me = lax.axis_index("ci")
 
@@ -134,7 +135,7 @@
 
     cols_w = min(2 * LANES, ci_n)
     group = 8
-    per = cols_w // LANES
+    per = cols_w // cut
 
     def shares(h):
         for first in range(0, planes, group):
@@ -152,7 +153,7 @@
                 c = h * per + q
                 for p in range(group):
                     acc[c, place(first + p, orders[c])] = total[
-                        p * PLANE:(p + 1) * PLANE, q * LANES:(q + 1) * LANES
+                        p * PLANE:(p + 1) * PLANE, q * cut:(q + 1) * cut
                     ]
 
     def where_at(c, s):
@@ -182,7 +183,7 @@
             acc[c, spot] = acc[c, spot] + recvs[s][c]
         else:
             block = acc[c, where_at(c, s + 1)] + recvs[s][c, 0]
-            ingrad_ref[:, c * LANES:(c + 1) * LANES] = block.astype(ingrad_ref.dtype)
+            ingrad_ref[:, c * cut:(c + 1) * cut] = block.astype(ingrad_ref.dtype)
 
     def step(c, s):
         arrive(c, s)
@@ -202,7 +203,7 @@
         response_tile(at)
     for c in lead[1:]:
         arrive(c, 0)
-        if c == lead[1]:
+        if c in lead[1:2]:
             begin(c, 1)
 
     lane = lax.broadcasted_iota(jnp.int32, (co_n, cells), 1)
@@ -307,7 +308,8 @@
     ci_n, cells = features.shape
     co_n, half = out_grad.shape
     stages = n_co.bit_length() - 1
-    chunks = ci_n // LANES
+    cut = min(2 * LANES, ci_n)
+    chunks = ci_n // cut
     near = tuple(range(stages))
     far = (0,) + tuple(range(2, stages)) + (1,)
     orders = tuple(far if c == 1 else near for c in range(chunks))
@@ -320,8 +322,8 @@
         pltpu.VMEM((rows_w + wide - 3 * co_n, ci_n), jnp.bfloat16),
         pltpu.VMEM((n_ci, co_n, half), jnp.bfloat16),
         pltpu.VMEM((3, cells + 2 * PLANE, wide), jnp.bfloat16),
-        pltpu.VMEM((chunks, n_co, PLANE, LANES), jnp.float32),
-        [pltpu.VMEM((chunks, n_co >> (s + 1), PLANE, LANES), jnp.float32) for s in range(stages)],
+        pltpu.VMEM((chunks, n_co, PLANE, cut), jnp.float32),
+        [pltpu.VMEM((chunks, n_co >> (s + 1), PLANE, cut), jnp.float32) for s in range(stages)],
         pltpu.VMEM((3, co_n, cells), jnp.float32),
         pltpu.VMEM((n_ci, co_n, half), jnp.float32),
         pltpu.VMEM((other, co_n, half), jnp.float32),

time: 36.3 us -> 36.5 us (level)
  no operation moved by 1% of the time
where the time goes in v6:
time: 36.5 us; the launch traced here: 36.4 us
  Pallas kernels  35.8 us (98%)
  between operations  0.64 us (2%)
    pallas_call x1, Pallas kernels, body(): pl.pallas_call(functools.partial(kernel, n_co, n_ci, orders), out_shape=s...  33.7 us
    pallas_call x1, Pallas kernels, body(): pl.pallas_call(hand_over, out_shape=shapes, in_specs=[vmem] * 3, out_spec...  2.07 us

profile of v6, /device:TPU:0, one launch (start us, length us, event | category | flops | bytes accessed | tf_op | source)
XLA Modules:
  0.0 36.4 jit_solution(1099999775155483072)
XLA Ops:
  0.6 33.7 %shard_map.58 = (bf16[64,512]{1,0:T(8,128)(2,1)S(1)}, bf16[64,512]{1,0:T(8,128)(2,1)S(1)}, f32[1728,512]{1,0:T(8,128)S(1)}) custom-call(bf16[512,1024]{1,0:T(8,128)(2,1)} %f_hbm.1, bf16[1728,512]{1,0:T(8,128)(2,1)} %bitcast.4, bf16[64,512]{1,0:T(8,128)(2,1)} %g_hbm.1), custom_call_target="tpu_custom_call" | custom-call | flops 5435817984 | bytes 7077888 | tf_op jit(solution)/shard_map/pallas_call | solution.py:342
  34.3 2.1 %shard_map.59 = (bf16[64,512]{1,0:T(8,128)(2,1)}, bf16[64,512]{1,0:T(8,128)(2,1)}, f32[1728,512]{1,0:T(8,128)}) custom-call(bf16[64,512]{1,0:T(8,128)(2,1)S(1)} %get-tuple-element.9.r_ref, bf16[64,512]{1,0:T(8,128)(2,1)S(1)} %get-tuple-element.10.i_ref, f32[1728,512]{1,0:T(8,128)S(1)} %get-tuple-element.11.w_ref), custom_call_target="tpu_custom_call" | custom-call | bytes 7077888 | tf_op jit(solution)/shard_map/pallas_call | solution.py:355
